TPU v7x, 32 devices: a whole 2x2x4 slice. The times are simulated.
32 devices in a mesh: chan: 8 (over z, y), tm: 4 (over x, core).
Axes of the slice: x: 2, y: 2, z: 4, core: 2. Of those that a mesh axis runs over, the one named last changes fastest.
Arguments:
- raw: float32 [2, 256, 1024], P(None, 'chan', 'tm'), may hold values from -40 to 40
- alive: int32 [256], P(('chan', 'tm')), may hold values 0 or 1
- seg_start: int32 [2], replicated, may hold values from 0 to 256, as said below
- norm_half: int32 [256], P(('chan', 'tm')), may hold values from 32 to 64, as said below
Outputs:
- corr: bfloat16 [256, 129, 256], P(('chan', 'tm'))
Inputs may be any that keep to these rules, and one draw needn't show every extreme that they name: `seg_start`: some segment starts exactly 256 samples into its window. `norm_half`: some channel has half-length 32 and some 64.
All inputs are finite; a program needn't handle non-finite values. No bound on the sum of `alive` on one device may be relied on, other than what follows from the above.
Results may differ from a plain program's by a relative error of at most 0.02.
Values may be sent and summed in bfloat16 or wider, within the bound.
A program may use at most 64 MiB of HBM per device.

v0:
```python
import math

import jax
import jax.numpy as jnp
import ml_dtypes
import numpy as np
from jax import lax
from jax.experimental import pallas as pl
from jax.experimental.pallas import tpu as pltpu
from jax.sharding import PartitionSpec as P

LAG = 64


widest = 64
smooth_half = 32
tiny = 1e-05
radix = 128


def window_mean(signal, half_width):
    length = signal.shape[2]
    half = half_width[None, :, None]
    width = 2 * half + 1
    power = jnp.pad(jnp.abs(signal), ((0, 0), (0, 0), (widest, widest)))

    def ahead(value, by):
        return jnp.pad(value[:, :, by:], ((0, 0), (0, 0), (0, by)))

    total = jnp.zeros_like(power)
    span = 1
    while span <= 2 * widest + 1:
        total = jnp.where((width & span) != 0, power + ahead(total, span), total)
        power = power + ahead(power, span)
        span *= 2
    rest = widest - half
    span = 1
    while span <= widest:
        total = jnp.where((rest & span) != 0, ahead(total, span), total)
        span *= 2
    return total[:, :, :length] / width.astype(jnp.float32)


def phase_table(row_total, col_total, modulus):
    product = (
        jnp.arange(row_total, dtype=jnp.int32)[:, None]
        * jnp.arange(col_total, dtype=jnp.int32)[None, :]
        % modulus
    )
    angle = product.astype(jnp.float32) * (2.0 * math.pi / modulus)
    return (jnp.cos(angle), jnp.sin(angle))


def forward_transform(signal, cos_q, sin_q, cos_p, sin_p, cos_t, sin_t):
    length = signal.shape[1]
    inner = length // radix
    highest = lax.Precision.HIGHEST
    grid = signal.reshape(-1, inner, radix)
    first_re = jnp.einsum("rqp,qk->rkp", grid, cos_q, precision=highest)
    first_im = -jnp.einsum("rqp,qk->rkp", grid, sin_q, precision=highest)
    turned_re = first_re * cos_t + first_im * sin_t
    turned_im = first_im * cos_t - first_re * sin_t
    out_re = jnp.einsum("rkp,pj->rjk", turned_re, cos_p, precision=highest) + jnp.einsum(
        "rkp,pj->rjk", turned_im, sin_p, precision=highest
    )
    out_im = jnp.einsum("rkp,pj->rjk", turned_im, cos_p, precision=highest) - jnp.einsum(
        "rkp,pj->rjk", turned_re, sin_p, precision=highest
    )
    return (out_re.reshape(-1, length), out_im.reshape(-1, length))


def inverse_real(spec_re, spec_im, cos_q, sin_q, cos_p, sin_p, cos_t, sin_t):
    length = spec_re.shape[1]
    inner = length // radix
    highest = lax.Precision.HIGHEST
    grid_re = spec_re.reshape(-1, radix, inner)
    grid_im = spec_im.reshape(-1, radix, inner)
    first_re = jnp.einsum("rjk,jp->rkp", grid_re, cos_p, precision=highest) - jnp.einsum(
        "rjk,jp->rkp", grid_im, sin_p, precision=highest
    )
    first_im = jnp.einsum("rjk,jp->rkp", grid_im, cos_p, precision=highest) + jnp.einsum(
        "rjk,jp->rkp", grid_re, sin_p, precision=highest
    )
    turned_re = first_re * cos_t - first_im * sin_t
    turned_im = first_im * cos_t + first_re * sin_t
    result = jnp.einsum("rkp,kq->rqp", turned_re, cos_q, precision=highest) - jnp.einsum(
        "rkp,kq->rqp", turned_im, sin_q, precision=highest
    )
    return result.reshape(-1, length)


def whiten(normed):
    segs, rows, length = normed.shape
    inner = length // radix
    cos_q, sin_q = phase_table(inner, inner, inner)
    cos_p, sin_p = phase_table(radix, radix, radix)
    cos_t, sin_t = phase_table(inner, radix, length)
    spec_re, spec_im = forward_transform(
        normed.reshape(-1, length), cos_q, sin_q, cos_p, sin_p, cos_t, sin_t
    )
    magnitude = jnp.sqrt(spec_re * spec_re + spec_im * spec_im)
    circular = jnp.concatenate(
        [magnitude[:, length - smooth_half :], magnitude, magnitude[:, :smooth_half]], axis=1
    )
    running = jnp.cumsum(circular, axis=1)
    running = jnp.concatenate([jnp.zeros((running.shape[0], 1), jnp.float32), running], axis=1)
    span_bins = 2 * smooth_half + 1
    smooth = (running[:, span_bins:] - running[:, :-span_bins]) / span_bins
    bins = jnp.arange(length, dtype=jnp.int32)
    folded = jnp.minimum(bins, length - bins)
    band = ((folded >= length // 250) & (folded <= 2 * length // 5)).astype(jnp.float32)
    gain = band[None, :] / (smooth + tiny)
    traces = inverse_real(spec_re * gain, spec_im * gain, cos_q, sin_q, cos_p, sin_p, cos_t, sin_t)
    return (traces * (1.0 / math.sqrt(length))).reshape(segs, rows, length).astype(jnp.bfloat16)


def normalised(gathered, alive, seg_start, norm_half):
    segs, rows, length = gathered.shape
    gathered = gathered * alive.astype(jnp.float32)[None, :, None]
    pieces = []
    for segment in range(segs):
        padded = jnp.pad(gathered[segment], ((0, 0), (0, length)))
        pieces.append(lax.dynamic_slice_in_dim(padded, seg_start[segment], length, axis=1))
    signal = jnp.stack(pieces, axis=0)
    return signal / (window_mean(signal, norm_half) + tiny)


def gathered_plan(raw, alive, seg_start, norm_half):
    segs = raw.shape[0]
    rows = alive.shape[0]
    lag_count = 2 * LAG + 1
    device = lax.axis_index("chan") * lax.axis_size("tm") + lax.axis_index("tm")
    pieces = lax.all_to_all(raw, "tm", split_axis=1, concat_axis=2, tiled=True)
    white = whiten(normalised(pieces, alive, seg_start, norm_half))
    length = white.shape[2]
    everyone = lax.all_gather(white, ("chan", "tm"), axis=1, tiled=True)
    padded = jnp.pad(white, ((0, 0), (0, 0), (LAG, LAG)))
    toeplitz = jnp.stack(
        [padded[:, :, 2 * LAG - lag : 2 * LAG - lag + length] for lag in range(lag_count)], axis=2
    )
    total = jnp.einsum("silt,sjt->ilj", toeplitz, everyone, preferred_element_type=jnp.float32)
    row_ids = device * rows + jnp.arange(rows, dtype=jnp.int32)
    col_ids = jnp.arange(everyone.shape[1], dtype=jnp.int32)
    keep = row_ids[:, None, None] != col_ids[None, None, :]
    scaled = total * (1.0 / math.sqrt(segs * length))
    return jnp.where(keep, scaled, 0.0).astype(jnp.bfloat16)


MESH = pl.DeviceIdType.MESH
lag_rows = 144


def two_parts(table):
    high = table.astype(ml_dtypes.bfloat16)
    low = (table - high.astype(np.float64)).astype(ml_dtypes.bfloat16)
    return np.stack([high, low])


def transform_tables(length):
    half, quarter = length // 2, length // 4
    moments = np.arange(half)
    low_bin, high_bin = length // 250, 2 * length // 5
    ahead, back = [], []
    for parity in range(2):
        bins = 2 * np.arange(quarter) + parity
        angle = 2.0 * np.pi * ((moments[:, None] * bins[None, :]) % length) / length
        ahead.append(np.concatenate([np.cos(angle), -np.sin(angle)], axis=1))
        back.append(np.concatenate([np.cos(angle), -np.sin(angle)], axis=1).T)
    order = np.concatenate([np.arange(0, half, 2), np.arange(1, half, 2)])
    place = np.empty(half, np.int64)
    place[order] = np.arange(half)
    mean = np.zeros((half, half), np.float32)
    for column, bin_index in enumerate(order):
        if low_bin <= bin_index <= high_bin:
            for offset in range(-smooth_half, smooth_half + 1):
                mean[place[abs(bin_index + offset)], column] += 1.0
    return (
        two_parts(np.stack(ahead)),
        two_parts(np.stack(back)),
        mean.astype(ml_dtypes.bfloat16),
    )


def three_parts(value):
    high = value.astype(jnp.bfloat16)
    rest = value - high.astype(jnp.float32)
    middle = rest.astype(jnp.bfloat16)
    low = (rest - middle.astype(jnp.float32)).astype(jnp.bfloat16)
    return jnp.concatenate([high, middle, low], axis=0)


def split_dot(parts, table):
    rows = parts.shape[0] // 3
    result = jnp.dot(parts, table, preferred_element_type=jnp.float32)
    return result[2 * rows :] + result[rows : 2 * rows] + result[:rows]


def table_dot(value, high, low):
    parts = three_parts(value)
    return split_dot(parts, low) + split_dot(parts, high)


def turned(value, by):
    length = value.shape[1]
    return pltpu.roll(value, by % length, 1)


def normed_rows(records, start, alive, half):
    rows, length = records.shape
    signal = records * alive
    bit = 1
    while bit <= length // 4:
        signal = jnp.where((start & bit) != 0, turned(signal, -bit), signal)
        bit *= 2
    lane = lax.broadcasted_iota(jnp.int32, (rows, length), 1)
    signal = jnp.where(lane + start < length, signal, 0.0)
    power = jnp.concatenate([jnp.abs(signal), jnp.zeros((rows, 2 * widest), jnp.float32)], axis=1)
    width = 2 * half + 1
    total = power
    bit = 1
    while bit < 2 * widest:
        power = power + turned(power, -bit)
        bit *= 2
        total = jnp.where((width & bit) != 0, power + turned(total, -bit), total)
    bit = 1
    while bit <= widest:
        total = jnp.where((half & bit) != 0, turned(total, bit), total)
        bit *= 2
    level = total[:, :length] / width.astype(jnp.float32)
    return signal / (level + tiny)


def whiten_rows(normed, ahead, back, mean):
    length = normed.shape[1]
    half, quarter = length // 2, length // 4
    left, right = normed[:, :half], normed[:, half:]
    even = table_dot(left + right, ahead[0, 0], ahead[1, 0])
    odd = table_dot(left - right, ahead[0, 1], ahead[1, 1])
    even_power = even * even
    odd_power = odd * odd
    magnitude = jnp.sqrt(
        jnp.concatenate(
            [
                even_power[:, :quarter] + even_power[:, quarter:],
                odd_power[:, :quarter] + odd_power[:, quarter:],
            ],
            axis=1,
        )
    )
    smooth = split_dot(three_parts(magnitude), mean) / (2 * smooth_half + 1)
    place = lax.broadcasted_iota(jnp.int32, smooth.shape, 1)
    bins = jnp.where(place < quarter, 2 * place, 2 * (place - quarter) + 1)
    keep = (bins >= length // 250) & (bins <= 2 * length // 5)
    gain = jnp.where(keep, 1.0 / (smooth + tiny), 0.0)
    even_gain, odd_gain = gain[:, :quarter], gain[:, quarter:]
    even = even * jnp.concatenate([even_gain, even_gain], axis=1)
    odd = odd * jnp.concatenate([odd_gain, odd_gain], axis=1)
    even = table_dot(even, back[0, 0], back[1, 0])
    odd = table_dot(odd, back[0, 1], back[1, 1])
    return jnp.concatenate([even + odd, even - odd], axis=1) * (2.0 / math.sqrt(length))


def fill_lags(white, target, slot):
    rows, length = white.shape
    ring = jnp.concatenate([white, jnp.zeros((rows, 2 * LAG), jnp.float32)], axis=1)
    ring = turned(ring, -LAG)
    for row in range(rows):
        spread = jnp.broadcast_to(ring[row : row + 1], (lag_rows, length + 2 * LAG))
        lagged = pltpu.roll(spread, 0, 1, stride=1, stride_axis=0)
        target[slot, row] = lagged[:, :length].astype(jnp.bfloat16)


def fused_kernel(
    raw, alive, seg_start, norm_half, ahead_hbm, back_hbm, mean_hbm, out,
    ahead, back, mean, table_sem, records, params, own, other, lagged, totals,
    raw_send, raw_recv, param_send, param_recv, rail_send, rail_recv, core_send, core_recv,
):
    chan, tm = lax.axis_index("chan"), lax.axis_index("tm")
    depth = lax.axis_size("chan") // 2
    groups = lax.axis_size("tm")
    z, y, x, core = chan // 2, chan % 2, tm // 2, tm % 2
    rows = alive.shape[0]
    pair = 2 * rows
    length = own.shape[2]
    blocks = own.shape[0]

    loads = [
        pltpu.make_async_copy(source, target, table_sem.at[index])
        for index, (source, target) in enumerate(
            [(ahead_hbm, ahead), (mean_hbm, mean), (back_hbm, back)]
        )
    ]
    for load in loads:
        load.start()

    others = [(chan, (tm + step) % groups) for step in range(1, groups)]
    along = [(((z + step) % depth) * 2 + y, tm) for step in range(1, depth)]
    plane = [
        (y, 1 - x),
        (1 - y, x),
        (1 - y, 1 - x),
    ]
    plane_devices = [(z * 2 + py, px * 2 + core) for py, px in plane]
    barrier = pltpu.get_barrier_semaphore()
    greeted = others + along + plane_devices[1:]
    for device in greeted:
        pl.semaphore_signal(barrier, inc=1, device_id=device, device_id_type=MESH)

    row_ids = lax.broadcasted_iota(jnp.int32, (rows, 128), 0)
    live = jnp.zeros((rows, 128), jnp.int32)
    half = jnp.zeros((rows, 128), jnp.int32)
    for row in range(rows):
        live = jnp.where(row_ids == row, alive[row], live)
        half = jnp.where(row_ids == row, norm_half[row], half)
    params[core] = jnp.concatenate([live, half], axis=0).astype(jnp.float32)
    pl.semaphore_wait(barrier, len(greeted))

    def remote(source, target, send, receive, device):
        return pltpu.make_async_remote_copy(
            src_ref=source, dst_ref=target, send_sem=send, recv_sem=receive,
            device_id=device, device_id_type=MESH,
        )

    started = []
    for step in range(1, groups):
        peer = (tm + step) % groups
        first = pl.multiple_of((peer // 2) * pair, pair)
        copy = remote(
            raw.at[peer % 2, pl.ds(first, pair)], records.at[tm],
            raw_send.at[step - 1], raw_recv.at[tm], (chan, peer),
        )
        copy.start()
        started.append(copy)
    partner = (chan, x * 2 + 1 - core)
    copy = remote(params.at[core], params.at[core], param_send, param_recv, partner)
    copy.start()
    started.append(copy)
    records[tm] = raw[core, pl.ds(pl.multiple_of(x * pair, pair), pair)]
    for step in range(1, groups):
        peer = (tm + step) % groups
        remote(
            records.at[peer], records.at[peer], raw_send.at[step - 1], raw_recv.at[peer],
            (chan, peer),
        ).wait_recv()
    remote(
        params.at[1 - core], params.at[1 - core], param_send, param_recv, partner
    ).wait_recv()

    gathered = jnp.concatenate([records[group] for group in range(groups)], axis=1)
    live = jnp.concatenate([params[0, :rows], params[1, :rows]], axis=0)[:, :1]
    half = jnp.concatenate([params[0, rows:], params[1, rows:]], axis=0)[:, :1]
    normed = normed_rows(gathered, seg_start[core], live, half.astype(jnp.int32))
    for load in loads:
        load.wait()
    white = whiten_rows(normed, ahead, back, mean[...]).astype(jnp.bfloat16)

    def block_of(bz, by, bx):
        return (bz * 2 + by) * 2 + bx

    def to_core(block):
        copy = remote(
            own.at[block], other.at[block], core_send.at[block], core_recv.at[block], partner
        )
        copy.start()
        started.append(copy)

    def to_plane(block, bz):
        for index, device in enumerate(plane_devices):
            copy = remote(
                own.at[block], own.at[block], rail_send.at[bz, index], rail_recv.at[block], device
            )
            copy.start()
            started.append(copy)

    def arrived(buffer, semaphores, block):
        remote(
            buffer.at[block], buffer.at[block], core_send.at[block], semaphores.at[block], partner
        ).wait_recv()

    mine = block_of(z, y, x)
    own[mine] = white
    for index, device in enumerate(along):
        copy = remote(
            own.at[mine], own.at[mine], rail_send.at[depth, index], rail_recv.at[mine], device
        )
        copy.start()
        started.append(copy)
    to_plane(mine, 0)
    to_core(mine)

    wide = white.astype(jnp.float32)
    fill_lags(jnp.where(core == 0, wide[:rows], wide[rows:]), lagged, 0)

    for step in range(1, depth):
        block = block_of((z + step) % depth, y, x)
        arrived(own, rail_recv, block)
        to_plane(block, step)
        to_core(block)

    arrived(other, core_recv, mine)
    wide = other[mine].astype(jnp.float32)
    fill_lags(jnp.where(core == 0, wide[:rows], wide[rows:]), lagged, 1)

    for step in range(depth):
        for py, px in plane:
            block = block_of((z + step) % depth, py, px)
            arrived(own, rail_recv, block)
            to_core(block)

    def lag_dot(slot, columns):
        return lax.dot_general(
            lagged[slot].reshape(rows * lag_rows, length),
            columns[...].reshape(blocks * pair, length),
            (((1,), (1,)), ((), ())),
            preferred_element_type=jnp.float32,
        )

    totals[...] = lag_dot(0, own)
    for step in range(depth):
        for py, px in [(y, x)] + plane:
            if step == 0 and px is x and py is y:
                continue
            arrived(other, core_recv, block_of((z + step) % depth, py, px))
    totals[...] += lag_dot(1, other)
    lag_count = out.shape[1]
    columns = lax.broadcasted_iota(jnp.int32, (lag_count, blocks * pair), 1)
    first = (chan * groups + tm) * rows
    scale = 1.0 / math.sqrt(2 * length)
    for row in range(rows):
        block = totals[row * lag_rows : row * lag_rows + lag_count]
        out[row] = jnp.where(columns != first + row, block * scale, 0.0).astype(jnp.bfloat16)
    for copy in started:
        copy.wait_send()


def fused_plan(raw, alive, seg_start, norm_half):
    segs, width, span = raw.shape
    groups, chans = lax.axis_size("tm"), lax.axis_size("chan")
    rows = alive.shape[0]
    length = span * groups
    depth = chans // 2
    blocks = chans * 2
    half = length // 2
    ahead, back, mean = transform_tables(length)
    vmem = pl.BlockSpec(memory_space=pltpu.VMEM)
    smem = pl.BlockSpec(memory_space=pltpu.SMEM)
    hbm = pl.BlockSpec(memory_space=pl.ANY)
    dma = pltpu.SemaphoreType.DMA
    return pl.pallas_call(
        fused_kernel,
        out_shape=jax.ShapeDtypeStruct((rows, 2 * LAG + 1, width * chans), jnp.bfloat16),
        in_specs=[vmem, smem, smem, smem, hbm, hbm, hbm],
        out_specs=vmem,
        scratch_shapes=[
            pltpu.VMEM((2, 2, half, half), jnp.bfloat16),
            pltpu.VMEM((2, 2, half, half), jnp.bfloat16),
            pltpu.VMEM((half, half), jnp.bfloat16),
            dma((3,)),
            pltpu.VMEM((groups, 2 * rows, span), jnp.float32),
            pltpu.VMEM((2, 2 * rows, 128), jnp.float32),
            pltpu.VMEM((blocks, 2 * rows, length), jnp.bfloat16),
            pltpu.VMEM((blocks, 2 * rows, length), jnp.bfloat16),
            pltpu.VMEM((2, rows, lag_rows, length), jnp.bfloat16),
            pltpu.VMEM((rows * lag_rows, width * chans), jnp.float32),
            dma((groups - 1,)),
            dma((groups,)),
            dma(()),
            dma(()),
            dma((depth + 1, 3)),
            dma((blocks,)),
            dma((blocks,)),
            dma((blocks,)),
        ],
        compiler_params=pltpu.CompilerParams(
            collective_id=0, has_side_effects=True, vmem_limit_bytes=48 * 1024 * 1024
        ),
        cost_estimate=pl.CostEstimate(
            flops=4 * rows * lag_rows * length * width * chans,
            bytes_accessed=6 * 1024 * 1024,
            transcendentals=0,
        ),
    )(raw, alive, seg_start, norm_half, ahead, back, mean)


def on_device(raw, alive, seg_start, norm_half):
    segs, width, span = raw.shape
    shape = (lax.axis_size("chan"), lax.axis_size("tm"), segs, alive.shape[0], span)
    if shape == (8, 4, 2, 8, 256):
        return fused_plan(raw, alive, seg_start, norm_half)
    return gathered_plan(raw, alive, seg_start, norm_half)


def solution(mesh):
    return jax.shard_map(
        on_device,
        mesh=mesh,
        in_specs=(P(None, "chan", "tm"), P(("chan", "tm")), P(), P(("chan", "tm"))),
        out_specs=P(("chan", "tm"), None, None),
        check_vma=False,
    )
```

profile of v0, /device:TPU:0, one launch (start us, length us, event | category | flops | bytes accessed | tf_op | source)
XLA Modules:
  0.0 33.8 jit_solution(9123723839120597653)
XLA Ops:
  0.0 0.0 copy-start
  0.0 1.6 %copy-done = bf16[2,2,512,512]{3,2,1,0:T(8,128)(2,1)S(1)} copy-done((bf16[2,2,512,512]{3,2,1,0:T(8,128)(2,1)S(1)}, bf16[2,2,512,512]{3,2,1,0:T(8,128)(2,1)}, u32[]{:S(2)}) %copy-start) | copy-done | bytes 2097176
  1.6 0.0 copy-start.1
  1.6 1.6 %copy-done.1 = bf16[2,2,512,512]{3,2,1,0:T(8,128)(2,1)S(1)} copy-done((bf16[2,2,512,512]{3,2,1,0:T(8,128)(2,1)S(1)}, bf16[2,2,512,512]{3,2,1,0:T(8,128)(2,1)}, u32[]{:S(2)}) %copy-start.1) | copy-done | bytes 2097176
  3.2 0.0 copy-start.2
  3.2 1.0 %copy-done.2 = bf16[512,512]{1,0:T(8,128)(2,1)S(1)} copy-done((bf16[512,512]{1,0:T(8,128)(2,1)S(1)}, bf16[512,512]{1,0:T(8,128)(2,1)}, u32[]{:S(2)}) %copy-start.2) | copy-done | bytes 524312
  4.2 0.0 copy-start.3
  4.2 0.8 %copy-done.3 = f32[2,32,256]{2,1,0:T(8,128)S(1)} copy-done((f32[2,32,256]{2,1,0:T(8,128)S(1)}, f32[2,32,256]{2,1,0:T(8,128)}, u32[]{:S(2)}) %copy-start.3) | copy-done | bytes 65560
  5.1 0.0 copy-start.4
  5.1 0.7 %copy-done.4 = s32[8]{0:T(128)S(1)} copy-done((s32[8]{0:T(128)S(1)}, s32[8]{0:T(128)}, u32[]{:S(2)}) %copy-start.4) | copy-done | bytes 56
  5.7 0.0 copy-start.5
  5.7 0.7 %copy-done.5 = s32[2]{0:T(128)S(1)} copy-done((s32[2]{0:T(128)S(1)}, s32[2]{0:T(128)}, u32[]{:S(2)}) %copy-start.5) | copy-done | bytes 32
  6.4 0.0 copy-start.6
  6.4 0.7 %copy-done.6 = s32[8]{0:T(128)S(1)} copy-done((s32[8]{0:T(128)S(1)}, s32[8]{0:T(128)}, u32[]{:S(2)}) %copy-start.6) | copy-done | bytes 56
  7.0 25.9 %shard_map.73 = bf16[8,129,256]{2,1,0:T(8,128)(2,1)S(1)} custom-call(f32[2,32,256]{2,1,0:T(8,128)S(1)} %copy-done.3, s32[8]{0:T(128)S(1)} %copy-done.4, s32[2]{0:T(128)S(1)} %copy-done.5, s32[8]{0:T(128)S(1)} %copy-done.6, bf16[2,2,512,512]{3,2,1,0:T(8,128)(2,1)S(1)} %copy-done.1, bf16[2,2,512,512]{3,2,1,0:T(8,128)(2,1)S(1)} %copy-done, ...), custom_call_target="tpu_custom_call" | custom-call | flops 1207959552 | bytes 6291456 | tf_op jit(solution)/shard_map/pallas_call | solution.py:449
  32.9 0.9 %copy.8 = bf16[8,129,256]{2,0,1:T(8,128)(2,1)} copy(bf16[8,129,256]{2,1,0:T(8,128)(2,1)S(1)} %shard_map.73) | data formatting | bytes 1056768 | tf_op jit(solution)/shard_map/pallas_call | solution.py:449
Async XLA Ops:
  0.0 1.6 %copy-start = (bf16[2,2,512,512]{3,2,1,0:T(8,128)(2,1)S(1)}, bf16[2,2,512,512]{3,2,1,0:T(8,128)(2,1)}, u32[]{:S(2)}) copy-start(bf16[2,2,512,512]{3,2,1,0:T(8,128)(2,1)} %constant.7.clone.back_hbm) | copy-start | bytes 6291460
  1.6 1.6 %copy-start.1 = (bf16[2,2,512,512]{3,2,1,0:T(8,128)(2,1)S(1)}, bf16[2,2,512,512]{3,2,1,0:T(8,128)(2,1)}, u32[]{:S(2)}) copy-start(bf16[2,2,512,512]{3,2,1,0:T(8,128)(2,1)} %constant.6.clone.ahead_hbm) | copy-start | bytes 6291460
  3.2 1.0 %copy-start.2 = (bf16[512,512]{1,0:T(8,128)(2,1)S(1)}, bf16[512,512]{1,0:T(8,128)(2,1)}, u32[]{:S(2)}) copy-start(bf16[512,512]{1,0:T(8,128)(2,1)} %constant.8.clone.mean_hbm) | copy-start | bytes 1572868
  4.2 0.8 %copy-start.3 = (f32[2,32,256]{2,1,0:T(8,128)S(1)}, f32[2,32,256]{2,1,0:T(8,128)}, u32[]{:S(2)}) copy-start(f32[2,32,256]{2,1,0:T(8,128)} %raw.1) | copy-start | bytes 196612
  5.1 0.7 %copy-start.4 = (s32[8]{0:T(128)S(1)}, s32[8]{0:T(128)}, u32[]{:S(2)}) copy-start(s32[8]{0:T(128)} %alive.1) | copy-start | bytes 100
  5.7 0.7 %copy-start.5 = (s32[2]{0:T(128)S(1)}, s32[2]{0:T(128)}, u32[]{:S(2)}) copy-start(s32[2]{0:T(128)} %seg_start.1) | copy-start | bytes 28
  6.4 0.7 %copy-start.6 = (s32[8]{0:T(128)S(1)}, s32[8]{0:T(128)}, u32[]{:S(2)}) copy-start(s32[8]{0:T(128)} %norm_half.1) | copy-start | bytes 100
where the time goes:
time: 34.1 us; the launch traced here: 33.8 us
  Pallas kernels  25.9 us (76%)
  local copies, waits for them, and re-layouts  7.92 us (23%)
    pallas_call x1, Pallas kernels, fused_plan(): pl.pallas_call(fused_kernel, out_shape=jax.ShapeDtypeStruct((rows, 2 * LA...  25.9 us
    unnamed x14, local copies, waits for them, and re-layouts  7.03 us
    pallas_call x1, local copies, waits for them, and re-layouts, fused_plan(): pl.pallas_call(fused_kernel, out_shape=jax.ShapeDtypeStruct((rows, 2 * LA...  0.9 us

commit v1 on v0

--- a/solution.py
+++ b/solution.py
@@ -147,7 +147,6 @@
 
 
 MESH = pl.DeviceIdType.MESH
-lag_rows = 144
 
 
 def two_parts(table):
@@ -264,15 +263,15 @@
     rows, length = white.shape
     ring = jnp.concatenate([white, jnp.zeros((rows, 2 * LAG), jnp.float32)], axis=1)
     ring = turned(ring, -LAG)
-    for row in range(rows):
-        spread = jnp.broadcast_to(ring[row : row + 1], (lag_rows, length + 2 * LAG))
-        lagged = pltpu.roll(spread, 0, 1, stride=1, stride_axis=0)
-        target[slot, row] = lagged[:, :length].astype(jnp.bfloat16)
+    both = jnp.concatenate([ring, turned(ring, 1)], axis=0).astype(jnp.bfloat16)
+    for step in range(LAG + 1):
+        lagged = turned(both, 2 * step) if step else both
+        target[slot, 2 * rows * step : 2 * rows * (step + 1)] = lagged[:, :length]
 
 
 def fused_kernel(
-    raw, alive, seg_start, norm_half, ahead_hbm, back_hbm, mean_hbm, out,
-    ahead, back, mean, table_sem, records, params, own, other, lagged, totals,
+    raw, alive_hbm, start_hbm, half_hbm, ahead_hbm, back_hbm, mean_hbm, out,
+    alive, seg_start, norm_half, small_sem, own_sem, ahead, back, mean, table_sem, records, params, own, other, lagged, totals,
     raw_send, raw_recv, param_send, param_recv, rail_send, rail_recv, core_send, core_recv,
 ):
     chan, tm = lax.axis_index("chan"), lax.axis_index("tm")
@@ -284,6 +283,17 @@
     length = own.shape[2]
     blocks = own.shape[0]
 
+    smalls = [
+        pltpu.make_async_copy(source, target, small_sem.at[index])
+        for index, (source, target) in enumerate(
+            [(alive_hbm, alive), (start_hbm, seg_start), (half_hbm, norm_half)]
+        )
+    ]
+    for load in smalls:
+        load.start()
+    mine_first = pl.multiple_of(x * pair, pair)
+    kept = pltpu.make_async_copy(raw.at[core, pl.ds(mine_first, pair)], records.at[tm], own_sem)
+    kept.start()
     loads = [
         pltpu.make_async_copy(source, target, table_sem.at[index])
         for index, (source, target) in enumerate(
@@ -306,6 +316,8 @@
     for device in greeted:
         pl.semaphore_signal(barrier, inc=1, device_id=device, device_id_type=MESH)
 
+    for load in smalls:
+        load.wait()
     row_ids = lax.broadcasted_iota(jnp.int32, (rows, 128), 0)
     live = jnp.zeros((rows, 128), jnp.int32)
     half = jnp.zeros((rows, 128), jnp.int32)
@@ -335,7 +347,7 @@
     copy = remote(params.at[core], params.at[core], param_send, param_recv, partner)
     copy.start()
     started.append(copy)
-    records[tm] = raw[core, pl.ds(pl.multiple_of(x * pair, pair), pair)]
+    kept.wait()
     for step in range(1, groups):
         peer = (tm + step) % groups
         remote(
@@ -364,13 +376,16 @@
         copy.start()
         started.append(copy)
 
-    def to_plane(block, bz):
-        for index, device in enumerate(plane_devices):
-            copy = remote(
-                own.at[block], own.at[block], rail_send.at[bz, index], rail_recv.at[block], device
-            )
-            copy.start()
-            started.append(copy)
+    def to_side(block, side, semaphore):
+        copy = remote(
+            own.at[block], own.at[block], semaphore, rail_recv.at[block], plane_devices[side]
+        )
+        copy.start()
+        started.append(copy)
+
+    def to_plane(block, step):
+        for side in range(2):
+            to_side(block, side, rail_send.at[step, side])
 
     def arrived(buffer, semaphores, block):
         remote(
@@ -402,14 +417,20 @@
     fill_lags(jnp.where(core == 0, wide[:rows], wide[rows:]), lagged, 1)
 
     for step in range(depth):
-        for py, px in plane:
-            block = block_of((z + step) % depth, py, px)
+        for side in range(2):
+            block = block_of((z + step) % depth, *plane[side])
             arrived(own, rail_recv, block)
+            if step % 2 == side:
+                to_side(block, 1 - side, rail_send.at[step, 2])
             to_core(block)
+    for step in range(depth):
+        block = block_of((z + step) % depth, *plane[2])
+        arrived(own, rail_recv, block)
+        to_core(block)
 
     def lag_dot(slot, columns):
         return lax.dot_general(
-            lagged[slot].reshape(rows * lag_rows, length),
+            lagged[slot],
             columns[...].reshape(blocks * pair, length),
             (((1,), (1,)), ((), ())),
             preferred_element_type=jnp.float32,
@@ -421,14 +442,13 @@
             if step == 0 and px is x and py is y:
                 continue
             arrived(other, core_recv, block_of((z + step) % depth, py, px))
-    totals[...] += lag_dot(1, other)
-    lag_count = out.shape[1]
-    columns = lax.broadcasted_iota(jnp.int32, (lag_count, blocks * pair), 1)
-    first = (chan * groups + tm) * rows
-    scale = 1.0 / math.sqrt(2 * length)
-    for row in range(rows):
-        block = totals[row * lag_rows : row * lag_rows + lag_count]
-        out[row] = jnp.where(columns != first + row, block * scale, 0.0).astype(jnp.bfloat16)
+    lag_count = out.shape[0]
+    shape = (lag_count * rows, blocks * pair)
+    ahead_by = lax.broadcasted_iota(jnp.int32, shape, 1) - (chan * groups + tm) * rows
+    same = ahead_by == lax.broadcasted_iota(jnp.int32, shape, 0) % rows
+    result = (totals[...] + lag_dot(1, other))[: lag_count * rows]
+    result = jnp.where(same, 0.0, result * (1.0 / math.sqrt(2 * length)))
+    out[...] = result.reshape(out.shape).astype(jnp.bfloat16)
     for copy in started:
         copy.wait_send()
 
@@ -441,17 +461,22 @@
     depth = chans // 2
     blocks = chans * 2
     half = length // 2
+    lag_rows = 2 * (LAG + 1) * rows
     ahead, back, mean = transform_tables(length)
     vmem = pl.BlockSpec(memory_space=pltpu.VMEM)
-    smem = pl.BlockSpec(memory_space=pltpu.SMEM)
-    hbm = pl.BlockSpec(memory_space=pl.ANY)
+    hbm = pl.BlockSpec(memory_space=pltpu.HBM)
     dma = pltpu.SemaphoreType.DMA
-    return pl.pallas_call(
+    corr = pl.pallas_call(
         fused_kernel,
-        out_shape=jax.ShapeDtypeStruct((rows, 2 * LAG + 1, width * chans), jnp.bfloat16),
-        in_specs=[vmem, smem, smem, smem, hbm, hbm, hbm],
+        out_shape=jax.ShapeDtypeStruct((2 * LAG + 1, rows, width * chans), jnp.bfloat16),
+        in_specs=[hbm] * 7,
         out_specs=vmem,
         scratch_shapes=[
+            pltpu.SMEM((rows,), jnp.int32),
+            pltpu.SMEM((segs,), jnp.int32),
+            pltpu.SMEM((rows,), jnp.int32),
+            dma((3,)),
+            dma(()),
             pltpu.VMEM((2, 2, half, half), jnp.bfloat16),
             pltpu.VMEM((2, 2, half, half), jnp.bfloat16),
             pltpu.VMEM((half, half), jnp.bfloat16),
@@ -460,8 +485,8 @@
             pltpu.VMEM((2, 2 * rows, 128), jnp.float32),
             pltpu.VMEM((blocks, 2 * rows, length), jnp.bfloat16),
             pltpu.VMEM((blocks, 2 * rows, length), jnp.bfloat16),
-            pltpu.VMEM((2, rows, lag_rows, length), jnp.bfloat16),
-            pltpu.VMEM((rows * lag_rows, width * chans), jnp.float32),
+            pltpu.VMEM((2, lag_rows, length), jnp.bfloat16),
+            pltpu.VMEM((lag_rows, width * chans), jnp.float32),
             dma((groups - 1,)),
             dma((groups,)),
             dma(()),
@@ -472,14 +497,15 @@
             dma((blocks,)),
         ],
         compiler_params=pltpu.CompilerParams(
-            collective_id=0, has_side_effects=True, vmem_limit_bytes=48 * 1024 * 1024
+            collective_id=0, has_side_effects=True, vmem_limit_bytes=60 * 1024 * 1024
         ),
         cost_estimate=pl.CostEstimate(
-            flops=4 * rows * lag_rows * length * width * chans,
+            flops=4 * lag_rows * length * width * chans,
             bytes_accessed=6 * 1024 * 1024,
             transcendentals=0,
         ),
     )(raw, alive, seg_start, norm_half, ahead, back, mean)
+    return jnp.transpose(corr, (1, 0, 2))
 
 
 def on_device(raw, alive, seg_start, norm_half):

time: 34.1 us -> 28.5 us (0.84)
  local copies, waits for them, and re-layouts: 7.92 us -> 1.87 us
  Pallas kernels: 25.9 us -> 26.5 us
    unnamed x14 -> x1, local copies, waits for them, and re-layouts: 7.03 us -> 1.87 us
    pallas_call x1 -> x0, local copies, waits for them, and re-layouts: 0.9 us -> none  [fused_plan(): pl.pallas_call(fused_kernel, out_shape=jax.ShapeDtypeStruct((rows, 2 * LA...]
    pallas_call x1, Pallas kernels: 25.9 us -> 26.5 us  [fused_plan(): pl.pallas_call(fused_kernel, out_shape=jax.ShapeDtypeStruct((2 * LAG + 1,...]
where the time goes in v1:
time: 28.5 us; the launch traced here: 28.4 us
  Pallas kernels  26.5 us (93%)
  local copies, waits for them, and re-layouts  1.87 us (7%)
    pallas_call x1, Pallas kernels, fused_plan(): pl.pallas_call(fused_kernel, out_shape=jax.ShapeDtypeStruct((2 * LAG + 1,...  26.5 us
    unnamed x1, local copies, waits for them, and re-layouts  1.87 us

profile of v1, /device:TPU:0, one launch (start us, length us, event | category | flops | bytes accessed | tf_op | source)
XLA Modules:
  0.0 28.4 jit_solution(8134656164181532239)
XLA Ops:
  0.0 26.5 %shard_map.73 = bf16[129,8,256]{2,1,0:T(8,128)(2,1)} custom-call(f32[2,32,256]{2,1,0:T(8,128)} %raw.1, s32[8]{0:T(128)} %alive_hbm.1, s32[2]{0:T(128)} %start_hbm.1, s32[8]{0:T(128)} %half_hbm.1, bf16[2,2,512,512]{3,2,1,0:T(8,128)(2,1)} %constant.6.clone.ahead_hbm, bf16[2,2,512,512]{3,2,1,0:T(8,128)(2,1)} %constant.7.clone.back_hbm, ...), custom_call_target="tpu_custom_call" | custom-call | flops 1090519040 | bytes 6291456 | tf_op jit(solution)/shard_map/pallas_call | solution.py:469
  26.5 1.9 %copy.9 = bf16[8,129,256]{2,0,1:T(8,128)(2,1)} copy(bf16[8,129,256]{2,0,1:T(8,128)(2,1)} %bitcast.1) | data formatting | bytes 1056768

commit v2 on v1

--- a/solution.py
+++ b/solution.py
@@ -300,11 +300,12 @@
             [(ahead_hbm, ahead), (mean_hbm, mean), (back_hbm, back)]
         )
     ]
-    for load in loads:
+    for load in loads[:2]:
         load.start()
 
+    near = [z, z + 1 - 2 * (z % 2), z + 2 - 4 * (z // 2), 3 - z]
     others = [(chan, (tm + step) % groups) for step in range(1, groups)]
-    along = [(((z + step) % depth) * 2 + y, tm) for step in range(1, depth)]
+    along = [(level * 2 + y, tm) for level in near[1:]]
     plane = [
         (y, 1 - x),
         (1 - y, x),
@@ -343,6 +344,7 @@
         )
         copy.start()
         started.append(copy)
+    loads[2].start()
     partner = (chan, x * 2 + 1 - core)
     copy = remote(params.at[core], params.at[core], param_send, param_recv, partner)
     copy.start()
@@ -407,7 +409,7 @@
     fill_lags(jnp.where(core == 0, wide[:rows], wide[rows:]), lagged, 0)
 
     for step in range(1, depth):
-        block = block_of((z + step) % depth, y, x)
+        block = block_of(near[step], y, x)
         arrived(own, rail_recv, block)
         to_plane(block, step)
         to_core(block)
@@ -418,13 +420,13 @@
 
     for step in range(depth):
         for side in range(2):
-            block = block_of((z + step) % depth, *plane[side])
+            block = block_of(near[step], *plane[side])
             arrived(own, rail_recv, block)
             if step % 2 == side:
                 to_side(block, 1 - side, rail_send.at[step, 2])
             to_core(block)
     for step in range(depth):
-        block = block_of((z + step) % depth, *plane[2])
+        block = block_of(near[step], *plane[2])
         arrived(own, rail_recv, block)
         to_core(block)
 
@@ -441,14 +443,14 @@
         for py, px in [(y, x)] + plane:
             if step == 0 and px is x and py is y:
                 continue
-            arrived(other, core_recv, block_of((z + step) % depth, py, px))
+            arrived(other, core_recv, block_of(near[step], py, px))
     lag_count = out.shape[0]
-    shape = (lag_count * rows, blocks * pair)
+    shape = (rows, blocks * pair)
     ahead_by = lax.broadcasted_iota(jnp.int32, shape, 1) - (chan * groups + tm) * rows
-    same = ahead_by == lax.broadcasted_iota(jnp.int32, shape, 0) % rows
-    result = (totals[...] + lag_dot(1, other))[: lag_count * rows]
-    result = jnp.where(same, 0.0, result * (1.0 / math.sqrt(2 * length)))
-    out[...] = result.reshape(out.shape).astype(jnp.bfloat16)
+    same = ahead_by == lax.broadcasted_iota(jnp.int32, shape, 0)
+    result = (totals[...] + lag_dot(1, other))[: lag_count * rows].reshape(out.shape)
+    result = jnp.where(same[None], 0.0, result * (1.0 / math.sqrt(2 * length)))
+    out[...] = result.astype(jnp.bfloat16)
     for copy in started:
         copy.wait_send()
 
@@ -463,12 +465,14 @@
     half = length // 2
     lag_rows = 2 * (LAG + 1) * rows
     ahead, back, mean = transform_tables(length)
+    operands = (raw, alive, seg_start, norm_half, ahead, back, mean)
+    operands = [jnp.asarray(operand) for operand in operands]
     vmem = pl.BlockSpec(memory_space=pltpu.VMEM)
     hbm = pl.BlockSpec(memory_space=pltpu.HBM)
     dma = pltpu.SemaphoreType.DMA
     corr = pl.pallas_call(
         fused_kernel,
-        out_shape=jax.ShapeDtypeStruct((2 * LAG + 1, rows, width * chans), jnp.bfloat16),
+        out_shape=pltpu.VMEM((2 * LAG + 1, rows, width * chans), jnp.bfloat16),
         in_specs=[hbm] * 7,
         out_specs=vmem,
         scratch_shapes=[
@@ -497,14 +501,14 @@
             dma((blocks,)),
         ],
         compiler_params=pltpu.CompilerParams(
-            collective_id=0, has_side_effects=True, vmem_limit_bytes=60 * 1024 * 1024
+            collective_id=0, has_side_effects=True, vmem_limit_bytes=48 * 1024 * 1024
         ),
         cost_estimate=pl.CostEstimate(
             flops=4 * lag_rows * length * width * chans,
             bytes_accessed=6 * 1024 * 1024,
             transcendentals=0,
         ),
-    )(raw, alive, seg_start, norm_half, ahead, back, mean)
+    )(*[pltpu.with_memory_space_constraint(operand, pltpu.HBM) for operand in operands])
     return jnp.transpose(corr, (1, 0, 2))
 
 

time: 28.5 us -> 26.8 us (0.940)
  local copies, waits for them, and re-layouts: 1.87 us -> 0.8 us
  Pallas kernels: 26.5 us -> 25.9 us
    unnamed x1, local copies, waits for them, and re-layouts: 1.87 us -> 0.8 us
    pallas_call x1, Pallas kernels: 26.5 us -> 25.9 us  [fused_plan(): pl.pallas_call(fused_kernel, out_shape=pltpu.VMEM((2 * LAG + 1, rows, wid...]
where the time goes in v2:
time: 26.8 us; the launch traced here: 26.7 us
  Pallas kernels  25.9 us (97%)
  local copies, waits for them, and re-layouts  0.8 us (3%)
    pallas_call x1, Pallas kernels, fused_plan(): pl.pallas_call(fused_kernel, out_shape=pltpu.VMEM((2 * LAG + 1, rows, wid...  25.9 us
    unnamed x1, local copies, waits for them, and re-layouts  0.8 us

profile of v2, /device:TPU:0, one launch (start us, length us, event | category | flops | bytes accessed | tf_op | source)
XLA Modules:
  0.0 26.7 jit_solution(10207222329503215577)
XLA Ops:
  0.0 25.9 %shard_map.73 = bf16[129,8,256]{2,1,0:T(8,128)(2,1)S(1)} custom-call(f32[2,32,256]{2,1,0:T(8,128)} %raw.1, s32[8]{0:T(128)} %alive_hbm.1, s32[2]{0:T(128)} %start_hbm.1, s32[8]{0:T(128)} %half_hbm.1, bf16[2,2,512,512]{3,2,1,0:T(8,128)(2,1)} %constant.6.clone.ahead_hbm, bf16[2,2,512,512]{3,2,1,0:T(8,128)(2,1)} %constant.7.clone.back_hbm, ...), custom_call_target="tpu_custom_call" | custom-call | flops 1090519040 | bytes 6291456 | tf_op jit(solution)/shard_map/pallas_call | solution.py:473
  25.9 0.8 %copy.9 = bf16[8,129,256]{2,0,1:T(8,128)(2,1)} copy(bf16[8,129,256]{2,0,1:T(8,128)(2,1)S(1)} %bitcast.1) | data formatting | bytes 1056768

commit v3 on v2

--- a/solution.py
+++ b/solution.py
@@ -204,28 +204,35 @@
     return pltpu.roll(value, by % length, 1)
 
 
+def window_sum(first, count, limit, way):
+    power = first
+    total = jnp.where((count & 1) != 0, power, 0.0)
+    bit = 1
+    while 2 * bit <= limit:
+        power = power + turned(power, way * bit)
+        bit *= 2
+        total = jnp.where((count & bit) != 0, power + turned(total, way * bit), total)
+    return total
+
+
 def normed_rows(records, start, alive, half):
     rows, length = records.shape
-    signal = records * alive
+    signal = records * jnp.concatenate([alive] * (length // 128), axis=1)
     bit = 1
     while bit <= length // 4:
-        signal = jnp.where((start & bit) != 0, turned(signal, -bit), signal)
-        bit *= 2
+        digit = (start // bit) % 4
+        one, two, three = (turned(signal, -bit * times) for times in (1, 2, 3))
+        signal = jnp.where(
+            digit == 0, signal, jnp.where(digit == 1, one, jnp.where(digit == 2, two, three))
+        )
+        bit *= 4
     lane = lax.broadcasted_iota(jnp.int32, (rows, length), 1)
     signal = jnp.where(lane + start < length, signal, 0.0)
     power = jnp.concatenate([jnp.abs(signal), jnp.zeros((rows, 2 * widest), jnp.float32)], axis=1)
-    width = 2 * half + 1
-    total = power
-    bit = 1
-    while bit < 2 * widest:
-        power = power + turned(power, -bit)
-        bit *= 2
-        total = jnp.where((width & bit) != 0, power + turned(total, -bit), total)
-    bit = 1
-    while bit <= widest:
-        total = jnp.where((half & bit) != 0, turned(total, bit), total)
-        bit *= 2
-    level = total[:, :length] / width.astype(jnp.float32)
+    half = jnp.concatenate([half] * (power.shape[1] // 128), axis=1)
+    total = window_sum(power, half + 1, widest + 1, -1)
+    total = total + window_sum(turned(power, 1), half, widest, 1)
+    level = total[:, :length] / (2 * half[:, :length] + 1).astype(jnp.float32)
     return signal / (level + tiny)
 
 
@@ -259,14 +266,19 @@
     return jnp.concatenate([even + odd, even - odd], axis=1) * (2.0 / math.sqrt(length))
 
 
-def fill_lags(white, target, slot):
+def both_lags(white):
     rows, length = white.shape
     ring = jnp.concatenate([white, jnp.zeros((rows, 2 * LAG), jnp.float32)], axis=1)
     ring = turned(ring, -LAG)
-    both = jnp.concatenate([ring, turned(ring, 1)], axis=0).astype(jnp.bfloat16)
-    for step in range(LAG + 1):
+    return jnp.concatenate([ring, turned(ring, 1)], axis=0).astype(jnp.bfloat16)
+
+
+def fill_lags(both, target, slot, first, last):
+    rows = both.shape[0]
+    length = target.shape[2]
+    for step in range(first, last):
         lagged = turned(both, 2 * step) if step else both
-        target[slot, 2 * rows * step : 2 * rows * (step + 1)] = lagged[:, :length]
+        target[slot, rows * step : rows * (step + 1)] = lagged[:, :length]
 
 
 def fused_kernel(
@@ -361,8 +373,8 @@
     ).wait_recv()
 
     gathered = jnp.concatenate([records[group] for group in range(groups)], axis=1)
-    live = jnp.concatenate([params[0, :rows], params[1, :rows]], axis=0)[:, :1]
-    half = jnp.concatenate([params[0, rows:], params[1, rows:]], axis=0)[:, :1]
+    live = jnp.concatenate([params[0, :rows], params[1, :rows]], axis=0)
+    half = jnp.concatenate([params[0, rows:], params[1, rows:]], axis=0)
     normed = normed_rows(gathered, seg_start[core], live, half.astype(jnp.int32))
     for load in loads:
         load.wait()
@@ -405,26 +417,36 @@
     to_plane(mine, 0)
     to_core(mine)
 
-    wide = white.astype(jnp.float32)
-    fill_lags(jnp.where(core == 0, wide[:rows], wide[rows:]), lagged, 0)
-
-    for step in range(1, depth):
+    def from_level(step):
         block = block_of(near[step], y, x)
         arrived(own, rail_recv, block)
         to_plane(block, step)
         to_core(block)
 
-    arrived(other, core_recv, mine)
-    wide = other[mine].astype(jnp.float32)
-    fill_lags(jnp.where(core == 0, wide[:rows], wide[rows:]), lagged, 1)
-
-    for step in range(depth):
+    def from_side(step):
         for side in range(2):
             block = block_of(near[step], *plane[side])
             arrived(own, rail_recv, block)
             if step % 2 == side:
                 to_side(block, 1 - side, rail_send.at[step, 2])
             to_core(block)
+
+    def own_rows(block):
+        wide = block.astype(jnp.float32)
+        return both_lags(jnp.where(core == 0, wide[:rows], wide[rows:]))
+
+    both = own_rows(white)
+    fill_lags(both, lagged, 0, 0, LAG // 2)
+    from_level(1)
+    fill_lags(both, lagged, 0, LAG // 2, LAG + 1)
+    from_side(0)
+    from_level(2)
+    from_side(1)
+    from_level(3)
+    arrived(other, core_recv, mine)
+    fill_lags(own_rows(other[mine]), lagged, 1, 0, LAG + 1)
+    from_side(2)
+    from_side(3)
     for step in range(depth):
         block = block_of(near[step], *plane[2])
         arrived(own, rail_recv, block)

time: 26.8 us -> 28.3 us (1.056)
  Pallas kernels: 25.9 us -> 27.4 us
    pallas_call x1, Pallas kernels: 25.9 us -> 27.4 us  [fused_plan(): pl.pallas_call(fused_kernel, out_shape=pltpu.VMEM((2 * LAG + 1, rows, wid...]
where the time goes in v3:
time: 28.3 us; the launch traced here: 28.2 us
  Pallas kernels  27.4 us (97%)
  local copies, waits for them, and re-layouts  0.8 us (3%)
    pallas_call x1, Pallas kernels, fused_plan(): pl.pallas_call(fused_kernel, out_shape=pltpu.VMEM((2 * LAG + 1, rows, wid...  27.4 us
    unnamed x1, local copies, waits for them, and re-layouts  0.8 us

profile of v3, /device:TPU:0, one launch (start us, length us, event | category | flops | bytes accessed | tf_op | source)
XLA Modules:
  0.0 28.2 jit_solution(776753051767246885)
XLA Ops:
  0.0 27.4 %shard_map.73 = bf16[129,8,256]{2,1,0:T(8,128)(2,1)S(1)} custom-call(f32[2,32,256]{2,1,0:T(8,128)} %raw.1, s32[8]{0:T(128)} %alive_hbm.1, s32[2]{0:T(128)} %start_hbm.1, s32[8]{0:T(128)} %half_hbm.1, bf16[2,2,512,512]{3,2,1,0:T(8,128)(2,1)} %constant.6.clone.ahead_hbm, bf16[2,2,512,512]{3,2,1,0:T(8,128)(2,1)} %constant.7.clone.back_hbm, ...), custom_call_target="tpu_custom_call" | custom-call | flops 1090519040 | bytes 6291456 | tf_op jit(solution)/shard_map/pallas_call | solution.py:495
  27.4 0.8 %copy.9 = bf16[8,129,256]{2,0,1:T(8,128)(2,1)} copy(bf16[8,129,256]{2,0,1:T(8,128)(2,1)S(1)} %bitcast.1) | data formatting | bytes 1056768

commit v4 on v3

--- a/solution.py
+++ b/solution.py
@@ -236,7 +236,7 @@
     return signal / (level + tiny)
 
 
-def whiten_rows(normed, ahead, back, mean):
+def whiten_rows(normed, ahead, back, mean, ready):
     length = normed.shape[1]
     half, quarter = length // 2, length // 4
     left, right = normed[:, :half], normed[:, half:]
@@ -261,6 +261,7 @@
     even_gain, odd_gain = gain[:, :quarter], gain[:, quarter:]
     even = even * jnp.concatenate([even_gain, even_gain], axis=1)
     odd = odd * jnp.concatenate([odd_gain, odd_gain], axis=1)
+    ready()
     even = table_dot(even, back[0, 0], back[1, 0])
     odd = table_dot(odd, back[0, 1], back[1, 1])
     return jnp.concatenate([even + odd, even - odd], axis=1) * (2.0 / math.sqrt(length))
@@ -376,9 +377,9 @@
     live = jnp.concatenate([params[0, :rows], params[1, :rows]], axis=0)
     half = jnp.concatenate([params[0, rows:], params[1, rows:]], axis=0)
     normed = normed_rows(gathered, seg_start[core], live, half.astype(jnp.int32))
-    for load in loads:
+    for load in loads[:2]:
         load.wait()
-    white = whiten_rows(normed, ahead, back, mean[...]).astype(jnp.bfloat16)
+    white = whiten_rows(normed, ahead, back, mean[...], loads[2].wait).astype(jnp.bfloat16)
 
     def block_of(bz, by, bx):
         return (bz * 2 + by) * 2 + bx
@@ -436,17 +437,13 @@
         return both_lags(jnp.where(core == 0, wide[:rows], wide[rows:]))
 
     both = own_rows(white)
-    fill_lags(both, lagged, 0, 0, LAG // 2)
-    from_level(1)
-    fill_lags(both, lagged, 0, LAG // 2, LAG + 1)
-    from_side(0)
-    from_level(2)
-    from_side(1)
-    from_level(3)
+    fill_lags(both, lagged, 0, 0, LAG + 1)
+    for step in range(1, depth):
+        from_level(step)
     arrived(other, core_recv, mine)
     fill_lags(own_rows(other[mine]), lagged, 1, 0, LAG + 1)
-    from_side(2)
-    from_side(3)
+    for step in range(depth):
+        from_side(step)
     for step in range(depth):
         block = block_of(near[step], *plane[2])
         arrived(own, rail_recv, block)

time: 28.3 us -> 26.2 us (0.926)
  Pallas kernels: 27.4 us -> 25.3 us
    pallas_call x1, Pallas kernels: 27.4 us -> 25.3 us  [fused_plan(): pl.pallas_call(fused_kernel, out_shape=pltpu.VMEM((2 * LAG + 1, rows, wid...]
where the time goes in v4:
time: 26.2 us; the launch traced here: 26.1 us
  Pallas kernels  25.3 us (97%)
  local copies, waits for them, and re-layouts  0.8 us (3%)
    pallas_call x1, Pallas kernels, fused_plan(): pl.pallas_call(fused_kernel, out_shape=pltpu.VMEM((2 * LAG + 1, rows, wid...  25.3 us
    unnamed x1, local copies, waits for them, and re-layouts  0.8 us

profile of v4, /device:TPU:0, one launch (start us, length us, event | category | flops | bytes accessed | tf_op | source)
XLA Modules:
  0.0 26.1 jit_solution(12616896866790695828)
XLA Ops:
  0.0 25.3 %shard_map.73 = bf16[129,8,256]{2,1,0:T(8,128)(2,1)S(1)} custom-call(f32[2,32,256]{2,1,0:T(8,128)} %raw.1, s32[8]{0:T(128)} %alive_hbm.1, s32[2]{0:T(128)} %start_hbm.1, s32[8]{0:T(128)} %half_hbm.1, bf16[2,2,512,512]{3,2,1,0:T(8,128)(2,1)} %constant.6.clone.ahead_hbm, bf16[2,2,512,512]{3,2,1,0:T(8,128)(2,1)} %constant.7.clone.back_hbm, ...), custom_call_target="tpu_custom_call" | custom-call | flops 1090519040 | bytes 6291456 | tf_op jit(solution)/shard_map/pallas_call | solution.py:492
  25.3 0.8 %copy.9 = bf16[8,129,256]{2,0,1:T(8,128)(2,1)} copy(bf16[8,129,256]{2,0,1:T(8,128)(2,1)S(1)} %bitcast.1) | data formatting | bytes 1056768

commit v5 on v4

--- a/solution.py
+++ b/solution.py
@@ -437,12 +437,16 @@
         return both_lags(jnp.where(core == 0, wide[:rows], wide[rows:]))
 
     both = own_rows(white)
-    fill_lags(both, lagged, 0, 0, LAG + 1)
-    for step in range(1, depth):
+    fill_lags(both, lagged, 0, 0, LAG // 2)
+    from_level(1)
+    fill_lags(both, lagged, 0, LAG // 2, LAG + 1)
+    for step in range(2, depth):
         from_level(step)
+    for step in range(2):
+        from_side(step)
     arrived(other, core_recv, mine)
     fill_lags(own_rows(other[mine]), lagged, 1, 0, LAG + 1)
-    for step in range(depth):
+    for step in range(2, depth):
         from_side(step)
     for step in range(depth):
         block = block_of(near[step], *plane[2])

time: 26.2 us -> 25.7 us (0.981)
  Pallas kernels: 25.3 us -> 24.8 us
    pallas_call x1, Pallas kernels: 25.3 us -> 24.8 us  [fused_plan(): pl.pallas_call(fused_kernel, out_shape=pltpu.VMEM((2 * LAG + 1, rows, wid...]
where the time goes in v5:
time: 25.7 us; the launch traced here: 25.6 us
  Pallas kernels  24.8 us (96%)
  local copies, waits for them, and re-layouts  0.8 us (3%)
    pallas_call x1, Pallas kernels, fused_plan(): pl.pallas_call(fused_kernel, out_shape=pltpu.VMEM((2 * LAG + 1, rows, wid...  24.8 us
    unnamed x1, local copies, waits for them, and re-layouts  0.8 us

profile of v5, /device:TPU:0, one launch (start us, length us, event | category | flops | bytes accessed | tf_op | source)
XLA Modules:
  0.0 25.6 jit_solution(15276677096010072275)
XLA Ops:
  0.0 24.8 %shard_map.73 = bf16[129,8,256]{2,1,0:T(8,128)(2,1)S(1)} custom-call(f32[2,32,256]{2,1,0:T(8,128)} %raw.1, s32[8]{0:T(128)} %alive_hbm.1, s32[2]{0:T(128)} %start_hbm.1, s32[8]{0:T(128)} %half_hbm.1, bf16[2,2,512,512]{3,2,1,0:T(8,128)(2,1)} %constant.6.clone.ahead_hbm, bf16[2,2,512,512]{3,2,1,0:T(8,128)(2,1)} %constant.7.clone.back_hbm, ...), custom_call_target="tpu_custom_call" | custom-call | flops 1090519040 | bytes 6291456 | tf_op jit(solution)/shard_map/pallas_call | solution.py:496
  24.8 0.8 %copy.9 = bf16[8,129,256]{2,0,1:T(8,128)(2,1)} copy(bf16[8,129,256]{2,0,1:T(8,128)(2,1)S(1)} %bitcast.1) | data formatting | bytes 1056768

commit v6 on v5

--- a/solution.py
+++ b/solution.py
@@ -437,17 +437,18 @@
         return both_lags(jnp.where(core == 0, wide[:rows], wide[rows:]))
 
     both = own_rows(white)
-    fill_lags(both, lagged, 0, 0, LAG // 2)
-    from_level(1)
-    fill_lags(both, lagged, 0, LAG // 2, LAG + 1)
-    for step in range(2, depth):
+    cuts = [(LAG + 1) * step // (depth - 1) for step in range(depth)]
+    for step in range(1, depth):
+        fill_lags(both, lagged, 0, cuts[step - 1], cuts[step])
         from_level(step)
     for step in range(2):
         from_side(step)
     arrived(other, core_recv, mine)
-    fill_lags(own_rows(other[mine]), lagged, 1, 0, LAG + 1)
+    both = own_rows(other[mine])
+    fill_lags(both, lagged, 1, 0, LAG // 2)
     for step in range(2, depth):
         from_side(step)
+    fill_lags(both, lagged, 1, LAG // 2, LAG + 1)
     for step in range(depth):
         block = block_of(near[step], *plane[2])
         arrived(own, rail_recv, block)

time: 25.7 us -> 26.3 us (1.023)
  Pallas kernels: 24.8 us -> 25.3 us
    pallas_call x1, Pallas kernels: 24.8 us -> 25.3 us  [fused_plan(): pl.pallas_call(fused_kernel, out_shape=pltpu.VMEM((2 * LAG + 1, rows, wid...]
where the time goes in v6:
time: 26.3 us; the launch traced here: 26.1 us
  Pallas kernels  25.3 us (96%)
  local copies, waits for them, and re-layouts  0.8 us (3%)
    pallas_call x1, Pallas kernels, fused_plan(): pl.pallas_call(fused_kernel, out_shape=pltpu.VMEM((2 * LAG + 1, rows, wid...  25.3 us
    unnamed x1, local copies, waits for them, and re-layouts  0.8 us

profile of v6, /device:TPU:0, one launch (start us, length us, event | category | flops | bytes accessed | tf_op | source)
XLA Modules:
  0.0 26.1 jit_solution(169007450979785474)
XLA Ops:
  0.0 25.3 %shard_map.73 = bf16[129,8,256]{2,1,0:T(8,128)(2,1)S(1)} custom-call(f32[2,32,256]{2,1,0:T(8,128)} %raw.1, s32[8]{0:T(128)} %alive_hbm.1, s32[2]{0:T(128)} %start_hbm.1, s32[8]{0:T(128)} %half_hbm.1, bf16[2,2,512,512]{3,2,1,0:T(8,128)(2,1)} %constant.6.clone.ahead_hbm, bf16[2,2,512,512]{3,2,1,0:T(8,128)(2,1)} %constant.7.clone.back_hbm, ...), custom_call_target="tpu_custom_call" | custom-call | flops 1090519040 | bytes 6291456 | tf_op jit(solution)/shard_map/pallas_call | solution.py:497
  25.3 0.8 %copy.9 = bf16[8,129,256]{2,0,1:T(8,128)(2,1)} copy(bf16[8,129,256]{2,0,1:T(8,128)(2,1)S(1)} %bitcast.1) | data formatting | bytes 1056768

commit v7 on v5

--- a/solution.py
+++ b/solution.py
@@ -442,11 +442,11 @@
     fill_lags(both, lagged, 0, LAG // 2, LAG + 1)
     for step in range(2, depth):
         from_level(step)
-    for step in range(2):
+    for step in range(3):
         from_side(step)
     arrived(other, core_recv, mine)
     fill_lags(own_rows(other[mine]), lagged, 1, 0, LAG + 1)
-    for step in range(2, depth):
+    for step in range(3, depth):
         from_side(step)
     for step in range(depth):
         block = block_of(near[step], *plane[2])

time: 25.7 us -> 26.2 us (1.019)
  Pallas kernels: 24.8 us -> 25.3 us
    pallas_call x1, Pallas kernels: 24.8 us -> 25.3 us  [fused_plan(): pl.pallas_call(fused_kernel, out_shape=pltpu.VMEM((2 * LAG + 1, rows, wid...]
where the time goes in v7:
time: 26.2 us; the launch traced here: 26.1 us
  Pallas kernels  25.3 us (97%)
  local copies, waits for them, and re-layouts  0.8 us (3%)
    pallas_call x1, Pallas kernels, fused_plan(): pl.pallas_call(fused_kernel, out_shape=pltpu.VMEM((2 * LAG + 1, rows, wid...  25.3 us
    unnamed x1, local copies, waits for them, and re-layouts  0.8 us

profile of v7, /device:TPU:0, one launch (start us, length us, event | category | flops | bytes accessed | tf_op | source)
XLA Modules:
  0.0 26.1 jit_solution(12478155075314369488)
XLA Ops:
  0.0 25.3 %shard_map.73 = bf16[129,8,256]{2,1,0:T(8,128)(2,1)S(1)} custom-call(f32[2,32,256]{2,1,0:T(8,128)} %raw.1, s32[8]{0:T(128)} %alive_hbm.1, s32[2]{0:T(128)} %start_hbm.1, s32[8]{0:T(128)} %half_hbm.1, bf16[2,2,512,512]{3,2,1,0:T(8,128)(2,1)} %constant.6.clone.ahead_hbm, bf16[2,2,512,512]{3,2,1,0:T(8,128)(2,1)} %constant.7.clone.back_hbm, ...), custom_call_target="tpu_custom_call" | custom-call | flops 1090519040 | bytes 6291456 | tf_op jit(solution)/shard_map/pallas_call | solution.py:496
  25.3 0.8 %copy.9 = bf16[8,129,256]{2,0,1:T(8,128)(2,1)} copy(bf16[8,129,256]{2,0,1:T(8,128)(2,1)S(1)} %bitcast.1) | data formatting | bytes 1056768
